TPU v7x, 128 devices: a whole 4x4x4 slice. The times are simulated.
128 devices in a mesh: occ: 4 (over y_hi, core), aux: 32 (over x, z, y_lo).
Axes of the slice: x: 4, y: 4 (y_hi: 2, y_lo: 2; y = y_hi * 2 + y_lo), z: 4, core: 2. Of those that a mesh axis runs over, the one named last changes fastest.
Arguments:
- three_index: bfloat16 [12000, 6, 1920], P('aux'), may hold values from -0.47851562 to 0.47851562
- occ_energy: float32 [6], replicated, may hold values from -1.5 to -0.3
- vir_energy: float32 [1920], replicated, may hold values from 0.25 to 2.95
- batch_table: int32 [6], replicated, may hold values from 0 to 5, each once
- orbital_order: int32 [6], replicated, may hold values from 0 to 5, each once
- occ_pair_int: bfloat16 [2, 2, 12000], P(None, None, 'aux'), may hold values from -0.03881836 to 0.03881836
- half_ao: bfloat16 [2, 12000, 4000], P(None, 'aux'), may hold values from -9.536743e-06 to 9.536743e-06
- vir_coeff: bfloat16 [4000, 1920], P('aux', 'occ'), may hold values from -0.09375 to 0.09375
Outputs:
- gamma: bfloat16 [12000, 2, 1920], P('aux', None, 'occ')
- orbital_gradient: float32 [2, 1920], P(None, ('occ', 'aux'))
Inputs may be any that keep to these rules, and one draw needn't show every extreme that they name: `batch_table`: a permutation of 0 to 5; its first 4 entries are the partner orbitals of the window. `orbital_order`: a permutation of 0 to 5; its first 2 entries are the orbitals whose amplitudes are formed.
All inputs are finite; a program needn't handle non-finite values.
Results may differ from a plain program's by a relative error of at most 0.019.
Values may be sent and summed in bfloat16 or wider, within the bound.
No kernel may reach another device: no remote copies, remote signals or barrier semaphores. Data moves between devices by JAX's collectives and lax.ppermute only.
A program may use at most 128 MiB of HBM per device.

v0:
```python
import jax
import jax.numpy as jnp
from jax import lax
from jax.sharding import Mesh
from jax.sharding import PartitionSpec as P

NI = 2
KH = 2
ROWS = 30
PAD = 32
AUX = ("x", "z", "yl")
OCC_AUX = ("yh", "core", "x", "z", "yl")
F32 = jnp.float32
BF16 = jnp.bfloat16


def ring(n, d):
    return [(i, (i + d) % n) for i in range(n)]


def up(v, axis):
    return lax.ppermute(v, axis, ring(4, 1))


def down(v, axis):
    return lax.ppermute(v, axis, ring(4, -1))


def dot(a, b, dims):
    return lax.dot_general(a, b, (dims, ((), ())), preferred_element_type=F32)


def ring_sum(v, axis):
    lo2, hi2 = v[2]
    got_up = up(lo2.astype(BF16), axis)
    got_down = down(hi2.astype(BF16), axis)
    one = jnp.concatenate([v[1][0] + got_up.astype(F32), v[1][1]]).astype(BF16)
    three = jnp.concatenate([v[3][0], v[3][1] + got_down.astype(F32)]).astype(BF16)
    from_below = up(one, axis)
    from_above = down(three, axis)
    own = jnp.concatenate([v[0][0], v[0][1]])
    return own + from_below.astype(F32) + from_above.astype(F32)


def ring_gather(v, axis):
    below = up(v, axis)
    above = down(v, axis)
    half = v.shape[0] // 2
    lo = up(below[:half], axis)
    hi = down(above[half:], axis)
    return [v, above, jnp.concatenate([lo, hi]), below]


def local(
    three_index,
    occ_energy,
    vir_energy,
    batch_table,
    orbital_order,
    occ_pair_int,
    half_ao,
    vir_coeff,
):
    nq, _, nvirt = three_index.shape
    yh, core, x, z, yl = (lax.axis_index(a) for a in OCC_AUX)
    own_a = (yh * 2 + core) * (nvirt // 4)
    by_orbital = jnp.transpose(three_index, (1, 0, 2))

    def orbital(i):
        return lax.dynamic_index_in_dim(by_orbital, i, 0, keepdims=False)

    def partner_orbital(half, k):
        return lax.dynamic_index_in_dim(batch_table, half * KH + k, 0, keepdims=False)

    pairs = []
    for h in range(2):
        for c in range(2):
            for t in range(2):
                src = h * 4 + c * 2 + t
                dst = (h if c == 0 else 1 - h) * 4 + c * 2 + (1 - t)
                pairs.append((src, dst))
    swap = lambda v: lax.ppermute(v, ("yh", "core", "yl"), pairs)
    right_sent = orbital(partner_orbital(1 - yl, core))
    right_first = swap(right_sent)
    right_second = lax.ppermute(right_first, "core", [(0, 1), (1, 0)])
    place = lax.broadcasted_iota(jnp.int32, (16 * PAD, 1), 0)
    dx, dz, r = (place // (4 * PAD), place // PAD % 4, place % PAD)
    chunk = (x + dx) % 4 * 4 + (z + dz) % 4
    virt = jnp.where(r < ROWS, chunk * ROWS + r, -nvirt)

    def left_rows(first):
        hot = (lax.broadcasted_iota(jnp.int32, (1, nvirt), 1) == virt + first).astype(BF16)
        both = [
            dot(hot, orbital(orbital_order[s]), ((1,), (1,))).astype(BF16).reshape(16, 1, PAD, nq)
            for s in range(NI)
        ]
        return jnp.concatenate(both, axis=1).reshape(16 * NI * PAD, nq)

    target_yh = jnp.where(core == 0, yh, 1 - yh)
    left_own = left_rows(own_a)
    left_sent = left_rows((target_yh * 2 + core) * (nvirt // 4))
    left_other = swap(left_sent)
    right_own = [orbital(partner_orbital(yl, k)) for k in range(KH)]
    right_other = [
        jnp.where(core == 0, right_first, right_second),
        jnp.where(core == 0, right_second, right_first),
    ]
    pair_flat = occ_pair_int.reshape(NI * NI, nq)
    g = [dot(pair_flat, half_ao[t], ((1,), (0,))) for t in range(NI)]
    cell = lambda u, v, t: g[t][u * NI + v]
    fock_terms = []
    for s in range(NI):
        fock_terms.append(2.0 * cell(0, 0, s) - cell(s, 0, 0))
        fock_terms.append(2.0 * (cell(0, 1, s) + cell(1, 0, s)) - cell(s, 1, 0) - cell(s, 0, 1))
        fock_terms.append(2.0 * cell(1, 1, s) - cell(s, 1, 1))
    fock_terms = jnp.stack(fock_terms)
    n_aux = lax.axis_size(AUX)
    tile = half_ao.shape[2] // n_aux
    fock_tile = lax.psum_scatter(
        fock_terms.reshape(6, n_aux, tile).transpose(1, 0, 2), AUX, scatter_dimension=0, tiled=False
    )
    vir_part = jnp.dot(fock_tile, vir_coeff.astype(F32), precision=lax.Precision.HIGHEST)
    share = vir_part.shape[1] // n_aux
    vir_own = lax.psum_scatter(
        vir_part.reshape(6, n_aux, share).transpose(1, 0, 2), AUX, scatter_dimension=0, tiled=False
    )
    pair_other = lax.ppermute(pair_flat, "yl", [(0, 1), (1, 0)])
    z_part = jnp.stack(
        [
            dot(pair_flat, right_own[k], ((1,), (0,)))
            + dot(pair_other, right_other[k], ((1,), (0,)))
            for k in range(KH)
        ]
    )
    z_sum = lax.psum(z_part, ("x", "z"))

    def by_block(left, swapped):
        blocks = left.reshape(4, 4, NI * PAD, nq)
        blocks = blocks.transpose(1, 0, 2, 3) if swapped else blocks
        return blocks.reshape(4, 2, 2 * NI * PAD, nq)

    summed = []
    for k, (first, second) in enumerate((("x", "z"), ("z", "x"))):
        lo_, oo_ = (by_block(left_own, k == 1), by_block(left_other, k == 1))
        v = {}
        for d in (2, 1, 3, 0):
            v[d] = [
                dot(lo_[d, h], right_own[k], ((1,), (0,)))
                + dot(oo_[d, h], right_other[k], ((1,), (0,)))
                for h in range(2)
            ]
        u = ring_sum(v, first).reshape(4, 2, PAD, nvirt)
        w = ring_sum([[u[d, 0], u[d, 1]] for d in range(4)], second)
        summed.append(w.reshape(NI, PAD, nvirt))
    own_chunk = x * 4 + z
    padded = jnp.concatenate([vir_energy, vir_energy[:2]])
    row_energy = lax.dynamic_slice_in_dim(padded, own_a + own_chunk * ROWS, PAD)
    left_energy = jnp.stack([occ_energy[orbital_order[s]] for s in range(NI)])
    amps = []
    for k in range(KH):
        e_k = lax.dynamic_index_in_dim(occ_energy, partner_orbital(yl, k), 0, keepdims=False)
        denominator = (
            row_energy[None, :, None] + vir_energy[None, None, :] - left_energy[:, None, None] - e_k
        )
        amps.append((-summed[k] / denominator).astype(BF16))
    wide = [a.astype(F32) for a in amps]
    entries = [-sum((jnp.sum(w[s] * w[t]) for w in wide)) for s, t in ((0, 0), (0, 1), (1, 1))]
    density = lax.psum(jnp.stack(entries), OCC_AUX)
    occ_rows = []
    for s in range(NI):
        row = jnp.zeros((PAD,), F32)
        for k in range(KH):
            for u in range(NI):
                row = row - jnp.sum(wide[k][u] * z_sum[k, u * NI + s][None, :], axis=1)
        occ_rows.append(row)
    occ_rows = jnp.stack(occ_rows)
    mine = lax.dynamic_slice_in_dim(occ_rows, yl * share, share, axis=1)
    theirs = lax.dynamic_slice_in_dim(occ_rows, (1 - yl) * share, share, axis=1)
    occ_side = mine + lax.ppermute(theirs, "yl", [(0, 1), (1, 0)])
    gammas = []
    for k, (first, second) in enumerate((("z", "x"), ("x", "z"))):
        own = jnp.concatenate(ring_gather(amps[k].reshape(NI * PAD, nvirt), first))
        blocks = ring_gather(own, second)
        parts = [
            [dot(b, right[k], ((1,), (1,))) for b in blocks] for right in (right_other, right_own)
        ]
        both = [jnp.concatenate(p).reshape(4, 4, NI * PAD, nq) for p in parts]
        if k == 1:
            both = [b.transpose(1, 0, 2, 3) for b in both]
        gammas.append(both)
    gamma_sent = (gammas[0][0] + gammas[1][0]).astype(BF16)
    gamma_got = lax.ppermute(gamma_sent, "yl", [(0, 1), (1, 0)])
    gamma_rows = (gammas[0][1] + gammas[1][1] + gamma_got.astype(F32)).astype(BF16)
    gamma_rows = gamma_rows.reshape(16, NI, PAD, nq)
    target = lax.broadcasted_iota(jnp.int32, (nvirt // 4, 1), 0)
    back = (target == virt.reshape(1, 16 * PAD)).astype(BF16)
    gamma_out = jnp.stack(
        [
            dot(back, gamma_rows[:, s].reshape(16 * PAD, nq), ((1,), (0,))).astype(BF16)
            for s in range(NI)
        ]
    )
    gamma_out = jnp.transpose(gamma_out, (2, 0, 1))
    weights = vir_own.reshape(NI, 3, share)
    gradient = occ_side + jnp.sum(weights * density[None, :, None], axis=1)
    return (gamma_out, gradient)


def solution(mesh):
    torus = Mesh(mesh.devices.reshape(2, 2, 4, 4, 2), OCC_AUX)
    occ = ("yh", "core")
    return jax.shard_map(
        local,
        mesh=torus,
        in_specs=(
            P(AUX, None, None),
            P(),
            P(),
            P(),
            P(),
            P(None, None, AUX),
            P(None, AUX, None),
            P(AUX, occ),
        ),
        out_specs=(P(AUX, None, occ), P(None, OCC_AUX)),
        check_vma=False,
    )
```

profile of v0, /device:TPU:0, one launch (start us, length us, event | category | flops | bytes accessed | tf_op | source)
XLA Modules:
  0.0 838.8 jit_solution(4391718574668692102)
XLA Ops:
  10.5 2.6 dynamic-slice_bitcast_fusion
  18.5 2.5 fusion.101
  21.8 2.5 fusion.104
  28.3 13.4 %fusion.165 = (bf16[1,375,4000]{2,0,1:T(2,128)(2,1)}, bf16[1,375,4000]{2,0,1:T(2,128)(2,1)}) fusion(bf16[2,375,4000]{2,0,1:T(2,128)(2,1)} %param.14), kind=kLoop, calls=%fused_computation.334 | loop fusion | bytes 12000000 | tf_op jit(solution)/shard_map/slice | solution.py:109
  41.7 13.8 %copy.135 = bf16[1,375,4000]{1,2,0:T(8,128)(2,1)S(1)} copy(bf16[1,375,4000]{2,0,1:T(2,128)(2,1)} %get-tuple-element.35) | data formatting | bytes 6000000
  56.4 13.9 %copy.134 = bf16[1,375,4000]{1,2,0:T(8,128)(2,1)S(1)} copy(bf16[1,375,4000]{2,0,1:T(2,128)(2,1)} %get-tuple-element.34) | data formatting | bytes 6000000
  74.2 2.5 fusion.95
  80.5 2.8 fusion.79
  83.3 2.8 fusion.81
  86.0 2.7 fusion.77
  88.8 2.7 fusion.71
  91.5 2.7 fusion.73
  94.2 2.7 fusion.75
  97.0 2.8 fusion.83
  99.7 2.7 fusion.85
  104.5 2.7 fusion.53
  107.2 2.8 fusion.55
  111.6 2.8 fusion.51
  114.5 2.8 fusion.45
  117.3 2.7 fusion.47
  120.0 2.8 fusion.49
  122.8 2.8 fusion.59
  128.4 2.8 fusion.57
  133.1 221.0 %all-reduce.4.cloned.1.call-done = f32[32,6,125]{2,1,0:T(8,128)} async-done(((f32[32,6,125]{2,1,0:T(8,128)}), f32[32,6,125]{2,1,0:T(8,128)}) %all-reduce.4.cloned.1.call-update) | async-done | bytes 96016
  356.1 154.6 %all-reduce.1 = f32[32,6,15]{2,1,0:T(8,128)S(1)} all-reduce(f32[32,6,15]{2,1,0:T(8,128)S(1)} %copy.133), channel_id=3, replica_groups=mesh['yh'=2,'core'=2,'x'=4,'z'=4,'yl'=2] {'x','z','yl'}, use_global_device_ids=true, to_apply=%region_10.11.clone | all-reduce | flops 2880 | bytes 23040
  519.9 3.2 collective-permute-start.5
  530.9 3.2 collective-permute-start.21
  537.5 70.3 %psum.14 = f32[2,4,1920]{2,1,0:T(4,128)S(1)} all-reduce(f32[2,4,1920]{2,1,0:T(4,128)S(1)} %pad_maximum_fusion.14), channel_id=1, replica_groups=mesh['yh'=2,'core'=2,'x'=4,'z'=4,'yl'=2] {'x','z'}, use_global_device_ids=true, to_apply=%region_0.1 | all-reduce | flops 15360 | bytes 122880 | tf_op jit(solution)/shard_map/psum | solution.py:135
  620.9 2.7 collective-permute-start.22
  623.5 3.2 collective-permute-done.4
  628.8 3.2 collective-permute-start.9
  635.7 3.2 collective-permute-start.25
  639.1 3.8 collective-permute-start.10
  643.1 3.3 collective-permute-start.26
  646.9 3.5 collective-permute-done.24
  654.3 3.3 collective-permute-start.27
  658.4 2.6 collective-permute-start.11
  668.1 65.9 %psum.15 = f32[3]{0:T(128)S(1)} all-reduce(f32[3]{0:T(128)S(1)} %pad_maximum_fusion.17), channel_id=1, replica_groups=mesh['yh'=2,'core'=2,'x'=4,'z'=4,'yl'=2] {'yh','core','x','z','yl'}, use_global_device_ids=true, to_apply=%region_17.18 | all-reduce | flops 3 | bytes 24 | tf_op jit(solution)/shard_map/psum | solution.py:168
  752.1 2.6 collective-permute-start.31
  758.3 2.7 collective-permute-start.15
  761.0 3.1 fusion.43
  764.1 2.9 fusion.69
  768.2 7.1 collective-permute-done.32
  775.6 3.3 collective-permute-start.34
  782.7 3.2 collective-permute-start.18
  805.9 3.0 copy.121
  808.9 2.6 fusion.32
  821.3 6.9 collective-permute-done.35
  (298 shorter events, 130.5 us)
Async XLA Ops:
  7.2 7.6 copy-start.42
  7.2 347.0 %all-reduce.4.cloned.1.call-start = ((), (), s32[]{:S(2)}) async-start(), calls=%async_computation | async-start | bytes 262144
  13.1 112.5 %collective-permute-start.1 = (bf16[375,1920]{1,0:T(8,128)(2,1)}, bf16[375,1920]{1,0:T(8,128)(2,1)}, u32[]{:S(2)}, u32[]{:S(2)}) collective-permute-start(bf16[375,1920]{1,0:T(8,128)(2,1)} %dynamic-slice_bitcast_fusion), channel_id=1, source_target_pairs={{0,1},{1,0},{32,97},{33,96},{64,65},{65,64},{96,33},{97,32},{2,3},... | collective-permute-start | bytes 4320008 | tf_op jit(solution)/shard_map/ppermute | solution.py:82
  26.0 485.3 %collective-permute-start = (bf16[1024,375]{0,1:T(8,128)(2,1)}, bf16[1024,375]{0,1:T(8,128)(2,1)}, u32[]{:S(2)}, u32[]{:S(2)}) collective-permute-start(bf16[1024,375]{0,1:T(8,128)(2,1)} %copy.104), channel_id=1, source_target_pairs={{0,1},{1,0},{32,97},{33,96},{64,65},{65,64},{96,33},{97,32},{2,3},... | collective-permute-start | bytes 2304008 | tf_op jit(solution)/shard_map/ppermute | solution.py:82
  26.4 510.5 %collective-permute-start.36 = (bf16[4,375]{1,0:T(4,128)(2,1)S(1)}, bf16[4,375]{1,0:T(4,128)(2,1)S(1)}, u32[]{:S(2)}, u32[]{:S(2)}) collective-permute-start(bf16[4,375]{1,0:T(4,128)(2,1)S(1)} %reshape.436), channel_id=1, source_target_pairs={{0,1},{1,0},{2,3},{3,2},{4,5},{5,4},{6,7},{7,6},{8,9},{9,8},{10,11... | collective-permute-start | bytes 9008 | tf_op jit(solution)/shard_map/ppermute | solution.py:127
  125.6 388.0 %collective-permute-start.2 = (bf16[375,1920]{1,0:T(8,128)(2,1)}, bf16[375,1920]{1,0:T(8,128)(2,1)}, u32[]{:S(2)}, u32[]{:S(2)}) collective-permute-start(bf16[375,1920]{1,0:T(8,128)(2,1)} %collective-permute-done.1), channel_id=1, source_target_pairs={{0,32},{32,0},{1,33},{33,1},{2,34},{34,2},{3,35},{35,3},{4,36},{36... | collective-permute-start | bytes 4320008 | tf_op jit(solution)/shard_map/ppermute | solution.py:85
  513.6 21.9 %copy-start.25 = (bf16[4,4,64,375]{3,2,1,0:T(8,128)(2,1)}, bf16[4,4,64,375]{3,2,1,0:T(8,128)(2,1)S(1)}, u32[]{:S(2)}) copy-start(bf16[4,4,64,375]{3,2,1,0:T(8,128)(2,1)S(1)} %copy.118) | copy-start | bytes 2304004
  517.5 92.3 %collective-permute-start.3 = (bf16[128,1920]{1,0:T(8,128)(2,1)}, bf16[128,1920]{1,0:T(8,128)(2,1)}, u32[]{:S(2)}, u32[]{:S(2)}) collective-permute-start(bf16[128,1920]{1,0:T(8,128)(2,1)} %fusion.13), channel_id=1, source_target_pairs={{0,8},{8,16},{16,24},{24,0},{1,9},{9,17},{17,25},{25,1},{2,10},{10... | collective-permute-start | bytes 1474568 | tf_op jit(solution)/shard_map/ppermute | solution.py:22
  519.9 91.6 %collective-permute-start.5 = (bf16[128,1920]{1,0:T(8,128)(2,1)}, bf16[128,1920]{1,0:T(8,128)(2,1)}, u32[]{:S(2)}, u32[]{:S(2)}) collective-permute-start(bf16[128,1920]{1,0:T(8,128)(2,1)} %fusion.17), channel_id=1, source_target_pairs={{0,24},{8,0},{16,8},{24,16},{1,25},{9,1},{17,9},{25,17},{2,26},{10... | collective-permute-start | bytes 1474568 | tf_op jit(solution)/shard_map/ppermute | solution.py:26
  528.4 88.1 %collective-permute-start.19 = (bf16[128,1920]{1,0:T(8,128)(2,1)}, bf16[128,1920]{1,0:T(8,128)(2,1)}, u32[]{:S(2)}, u32[]{:S(2)}) collective-permute-start(bf16[128,1920]{1,0:T(8,128)(2,1)} %fusion.19), channel_id=1, source_target_pairs={{0,2},{2,4},{4,6},{6,0},{1,3},{3,5},{5,7},{7,1},{8,10},{10,12},{12... | collective-permute-start | bytes 1474568 | tf_op jit(solution)/shard_map/ppermute | solution.py:22
  530.9 87.7 %collective-permute-start.21 = (bf16[128,1920]{1,0:T(8,128)(2,1)}, bf16[128,1920]{1,0:T(8,128)(2,1)}, u32[]{:S(2)}, u32[]{:S(2)}) collective-permute-start(bf16[128,1920]{1,0:T(8,128)(2,1)} %fusion.23), channel_id=1, source_target_pairs={{0,6},{2,0},{4,2},{6,4},{1,7},{3,1},{5,3},{7,5},{8,14},{10,8},{12,... | collective-permute-start | bytes 1474568 | tf_op jit(solution)/shard_map/ppermute | solution.py:26
  611.4 15.4 %collective-permute-start.4 = (bf16[256,1920]{1,0:T(8,128)(2,1)S(1)}, bf16[256,1920]{1,0:T(8,128)(2,1)S(1)}, u32[]{:S(2)}, u32[]{:S(2)}) collective-permute-start(bf16[256,1920]{1,0:T(8,128)(2,1)S(1)} %pad_maximum_fusion.4), channel_id=1, source_target_pairs={{0,8},{8,16},{16,24},{24,0},{1,9},{9,17},{17,25},{25,1},{2,10},{10... | collective-permute-start | bytes 2949128 | tf_op jit(solution)/shard_map/ppermute | solution.py:22
  614.1 14.2 %collective-permute-start.6 = (bf16[256,1920]{1,0:T(8,128)(2,1)S(1)}, bf16[256,1920]{1,0:T(8,128)(2,1)S(1)}, u32[]{:S(2)}, u32[]{:S(2)}) collective-permute-start(bf16[256,1920]{1,0:T(8,128)(2,1)S(1)} %pad_maximum_fusion.5), channel_id=1, source_target_pairs={{0,24},{8,0},{16,8},{24,16},{1,25},{9,1},{17,9},{25,17},{2,26},{10... | collective-permute-start | bytes 2949128 | tf_op jit(solution)/shard_map/ppermute | solution.py:26
  618.1 15.8 %collective-permute-start.20 = (bf16[256,1920]{1,0:T(8,128)(2,1)S(1)}, bf16[256,1920]{1,0:T(8,128)(2,1)S(1)}, u32[]{:S(2)}, u32[]{:S(2)}) collective-permute-start(bf16[256,1920]{1,0:T(8,128)(2,1)S(1)} %pad_maximum_fusion.6), channel_id=1, source_target_pairs={{0,2},{2,4},{4,6},{6,0},{1,3},{3,5},{5,7},{7,1},{8,10},{10,12},{12... | collective-permute-start | bytes 2949128 | tf_op jit(solution)/shard_map/ppermute | solution.py:22
  620.8 7.6 copy-start.23
  620.8 7.5 copy-start.24
  620.9 14.3 %collective-permute-start.22 = (bf16[256,1920]{1,0:T(8,128)(2,1)S(1)}, bf16[256,1920]{1,0:T(8,128)(2,1)S(1)}, u32[]{:S(2)}, u32[]{:S(2)}) collective-permute-start(bf16[256,1920]{1,0:T(8,128)(2,1)S(1)} %pad_maximum_fusion.7), channel_id=1, source_target_pairs={{0,6},{2,0},{4,2},{6,4},{1,7},{3,1},{5,3},{7,5},{8,14},{10,8},{12,... | collective-permute-start | bytes 2949128 | tf_op jit(solution)/shard_map/ppermute | solution.py:26
  628.7 6.5 copy-start.20
  628.8 10.1 %collective-permute-start.7 = (bf16[32,1920]{1,0:T(8,128)(2,1)S(1)}, bf16[32,1920]{1,0:T(8,128)(2,1)S(1)}, u32[]{:S(2)}, u32[]{:S(2)}) collective-permute-start(bf16[32,1920]{1,0:T(8,128)(2,1)S(1)} %get-tuple-element.50), channel_id=1, source_target_pairs={{0,2},{2,4},{4,6},{6,0},{1,3},{3,5},{5,7},{7,1},{8,10},{10,12},{12... | collective-permute-start | bytes 368648 | tf_op jit(solution)/shard_map/ppermute | solution.py:22
  628.8 10.1 %collective-permute-start.9 = (bf16[32,1920]{1,0:T(8,128)(2,1)S(1)}, bf16[32,1920]{1,0:T(8,128)(2,1)S(1)}, u32[]{:S(2)}, u32[]{:S(2)}) collective-permute-start(bf16[32,1920]{1,0:T(8,128)(2,1)S(1)} %get-tuple-element.51), channel_id=1, source_target_pairs={{0,6},{2,0},{4,2},{6,4},{1,7},{3,1},{5,3},{7,5},{8,14},{10,8},{12,... | collective-permute-start | bytes 368648 | tf_op jit(solution)/shard_map/ppermute | solution.py:26
  635.6 7.3 collective-permute-start.23
  635.7 7.2 collective-permute-start.25
  639.0 7.9 collective-permute-start.8
  639.1 7.8 collective-permute-start.10
  643.0 7.5 collective-permute-start.24
  643.1 7.4 collective-permute-start.26
  654.3 83.3 %collective-permute-start.27 = (bf16[64,1920]{1,0:T(8,128)(2,1)}, bf16[64,1920]{1,0:T(8,128)(2,1)}, u32[]{:S(2)}, u32[]{:S(2)}) collective-permute-start(bf16[64,1920]{1,0:T(8,128)(2,1)} %get-tuple-element.30), channel_id=1, source_target_pairs={{0,24},{8,0},{16,8},{24,16},{1,25},{9,1},{17,9},{25,17},{2,26},{10... | collective-permute-start | bytes 737288 | tf_op jit(solution)/shard_map/ppermute | solution.py:26
  657.7 77.1 %collective-permute-start.28 = (bf16[64,1920]{1,0:T(8,128)(2,1)}, bf16[64,1920]{1,0:T(8,128)(2,1)}, u32[]{:S(2)}, u32[]{:S(2)}) collective-permute-start(bf16[64,1920]{1,0:T(8,128)(2,1)} %get-tuple-element.30), channel_id=1, source_target_pairs={{0,8},{8,16},{16,24},{24,0},{1,9},{9,17},{17,25},{25,1},{2,10},{10... | collective-permute-start | bytes 737288 | tf_op jit(solution)/shard_map/ppermute | solution.py:22
  658.4 84.4 %collective-permute-start.11 = (bf16[64,1920]{1,0:T(8,128)(2,1)S(1)}, bf16[64,1920]{1,0:T(8,128)(2,1)}, u32[]{:S(2)}, u32[]{:S(2)}) collective-permute-start(bf16[64,1920]{1,0:T(8,128)(2,1)S(1)} %get-tuple-element.58), channel_id=1, source_target_pairs={{0,6},{2,0},{4,2},{6,4},{1,7},{3,1},{5,3},{7,5},{8,14},{10,8},{12,... | collective-permute-start | bytes 737288 | tf_op jit(solution)/shard_map/ppermute | solution.py:26
  661.0 79.0 %collective-permute-start.12 = (bf16[64,1920]{1,0:T(8,128)(2,1)S(1)}, bf16[64,1920]{1,0:T(8,128)(2,1)}, u32[]{:S(2)}, u32[]{:S(2)}) collective-permute-start(bf16[64,1920]{1,0:T(8,128)(2,1)S(1)} %get-tuple-element.58), channel_id=1, source_target_pairs={{0,2},{2,4},{4,6},{6,0},{1,3},{3,5},{5,7},{7,1},{8,10},{10,12},{12... | collective-permute-start | bytes 737288 | tf_op jit(solution)/shard_map/ppermute | solution.py:22
  668.1 66.0 %collective-permute-start.37 = (f32[2,15]{1,0:T(2,128)S(1)}, f32[2,15]{1,0:T(2,128)S(1)}, u32[]{:S(2)}, u32[]{:S(2)}) collective-permute-start(f32[2,15]{1,0:T(2,128)S(1)} %constant_dynamic-slice_fusion), channel_id=1, source_target_pairs={{0,1},{1,0},{2,3},{3,2},{4,5},{5,4},{6,7},{7,6},{8,9},{9,8},{10,11... | collective-permute-start | bytes 368 | tf_op jit(solution)/shard_map/ppermute | solution.py:179
  735.7 12.8 %collective-permute-start.29 = (bf16[32,1920]{1,0:T(8,128)(2,1)S(1)}, bf16[32,1920]{1,0:T(8,128)(2,1)S(1)}, u32[]{:S(2)}, u32[]{:S(2)}) collective-permute-start(bf16[32,1920]{1,0:T(8,128)(2,1)S(1)} %slice.420), channel_id=1, source_target_pairs={{0,8},{8,16},{16,24},{24,0},{1,9},{9,17},{17,25},{25,1},{2,10},{10... | collective-permute-start | bytes 368648 | tf_op jit(solution)/shard_map/ppermute | solution.py:22
  738.5 10.6 %collective-permute-start.30 = (bf16[32,1920]{1,0:T(8,128)(2,1)S(1)}, bf16[32,1920]{1,0:T(8,128)(2,1)S(1)}, u32[]{:S(2)}, u32[]{:S(2)}) collective-permute-start(bf16[32,1920]{1,0:T(8,128)(2,1)S(1)} %slice.421), channel_id=1, source_target_pairs={{0,24},{8,0},{16,8},{24,16},{1,25},{9,1},{17,9},{25,17},{2,26},{10... | collective-permute-start | bytes 368648 | tf_op jit(solution)/shard_map/ppermute | solution.py:26
  740.9 13.8 %collective-permute-start.13 = (bf16[32,1920]{1,0:T(8,128)(2,1)S(1)}, bf16[32,1920]{1,0:T(8,128)(2,1)S(1)}, u32[]{:S(2)}, u32[]{:S(2)}) collective-permute-start(bf16[32,1920]{1,0:T(8,128)(2,1)S(1)} %slice.392), channel_id=1, source_target_pairs={{0,2},{2,4},{4,6},{6,0},{1,3},{3,5},{5,7},{7,1},{8,10},{10,12},{12... | collective-permute-start | bytes 368648 | tf_op jit(solution)/shard_map/ppermute | solution.py:22
  743.7 11.6 %collective-permute-start.14 = (bf16[32,1920]{1,0:T(8,128)(2,1)S(1)}, bf16[32,1920]{1,0:T(8,128)(2,1)S(1)}, u32[]{:S(2)}, u32[]{:S(2)}) collective-permute-start(bf16[32,1920]{1,0:T(8,128)(2,1)S(1)} %slice.393), channel_id=1, source_target_pairs={{0,6},{2,0},{4,2},{6,4},{1,7},{3,1},{5,3},{7,5},{8,14},{10,8},{12,... | collective-permute-start | bytes 368648 | tf_op jit(solution)/shard_map/ppermute | solution.py:26
  751.4 23.9 %collective-permute-start.32 = (bf16[256,1920]{1,0:T(8,128)(2,1)}, bf16[256,1920]{1,0:T(8,128)(2,1)S(1)}, u32[]{:S(2)}, u32[]{:S(2)}) collective-permute-start(bf16[256,1920]{1,0:T(8,128)(2,1)} %constant_dynamic-update-slice_fusion.7), channel_id=1, source_target_pairs={{0,2},{2,4},{4,6},{6,0},{1,3},{3,5},{5,7},{7,1},{8,10},{10,12},{12... | collective-permute-start | bytes 2949128 | tf_op jit(solution)/shard_map/ppermute | solution.py:22
  752.1 23.4 %collective-permute-start.31 = (bf16[256,1920]{1,0:T(8,128)(2,1)}, bf16[256,1920]{1,0:T(8,128)(2,1)S(1)}, u32[]{:S(2)}, u32[]{:S(2)}) collective-permute-start(bf16[256,1920]{1,0:T(8,128)(2,1)} %constant_dynamic-update-slice_fusion.7), channel_id=1, source_target_pairs={{0,6},{2,0},{4,2},{6,4},{1,7},{3,1},{5,3},{7,5},{8,14},{10,8},{12,... | collective-permute-start | bytes 2949128 | tf_op jit(solution)/shard_map/ppermute | solution.py:26
  757.6 6.5 copy-start.6
  757.6 23.4 %collective-permute-start.16 = (bf16[256,1920]{1,0:T(8,128)(2,1)}, bf16[256,1920]{1,0:T(8,128)(2,1)S(1)}, u32[]{:S(2)}, u32[]{:S(2)}) collective-permute-start(bf16[256,1920]{1,0:T(8,128)(2,1)} %constant_dynamic-update-slice_fusion), channel_id=1, source_target_pairs={{0,8},{8,16},{16,24},{24,0},{1,9},{9,17},{17,25},{25,1},{2,10},{10... | collective-permute-start | bytes 2949128 | tf_op jit(solution)/shard_map/ppermute | solution.py:22
  758.3 23.5 %collective-permute-start.15 = (bf16[256,1920]{1,0:T(8,128)(2,1)}, bf16[256,1920]{1,0:T(8,128)(2,1)S(1)}, u32[]{:S(2)}, u32[]{:S(2)}) collective-permute-start(bf16[256,1920]{1,0:T(8,128)(2,1)} %constant_dynamic-update-slice_fusion), channel_id=1, source_target_pairs={{0,24},{8,0},{16,8},{24,16},{1,25},{9,1},{17,9},{25,17},{2,26},{10... | collective-permute-start | bytes 2949128 | tf_op jit(solution)/shard_map/ppermute | solution.py:26
  761.0 6.0 copy-start.5
  764.1 25.7 %slice-start = ((s8[8663040]{0:T(1024)(128)(4,1)}), s8[4194304]{0:T(1024)(128)(4,1)S(1)}, s32[]{:S(2)}) async-start(s8[8663040]{0:T(1024)(128)(4,1)} %bitcast.415), calls=%async_computation.1 | async-start | bytes 8388608
  767.6 22.3 %slice-start.1 = ((s8[8663040]{0:T(1024)(128)(4,1)}), s8[4194304]{0:T(1024)(128)(4,1)S(1)}, s32[]{:S(2)}) async-start(s8[8663040]{0:T(1024)(128)(4,1)} %bitcast.415), calls=%async_computation.2 | async-start | bytes 8388608
  775.4 20.0 %collective-permute-start.33 = (bf16[128,1920]{1,0:T(8,128)(2,1)S(1)}, bf16[128,1920]{1,0:T(8,128)(2,1)S(1)}, u32[]{:S(2)}, u32[]{:S(2)}) collective-permute-start(bf16[128,1920]{1,0:T(8,128)(2,1)S(1)} %slice.422), channel_id=1, source_target_pairs={{0,2},{2,4},{4,6},{6,0},{1,3},{3,5},{5,7},{7,1},{8,10},{10,12},{12... | collective-permute-start | bytes 1474568 | tf_op jit(solution)/shard_map/ppermute | solution.py:22
  775.6 19.9 %collective-permute-start.34 = (bf16[128,1920]{1,0:T(8,128)(2,1)S(1)}, bf16[128,1920]{1,0:T(8,128)(2,1)S(1)}, u32[]{:S(2)}, u32[]{:S(2)}) collective-permute-start(bf16[128,1920]{1,0:T(8,128)(2,1)S(1)} %slice.423), channel_id=1, source_target_pairs={{0,6},{2,0},{4,2},{6,4},{1,7},{3,1},{5,3},{7,5},{8,14},{10,8},{12,... | collective-permute-start | bytes 1474568 | tf_op jit(solution)/shard_map/ppermute | solution.py:26
  781.8 18.4 %collective-permute-start.17 = (bf16[128,1920]{1,0:T(8,128)(2,1)}, bf16[128,1920]{1,0:T(8,128)(2,1)}, u32[]{:S(2)}, u32[]{:S(2)}) collective-permute-start(bf16[128,1920]{1,0:T(8,128)(2,1)} %slice.394), channel_id=1, source_target_pairs={{0,8},{8,16},{16,24},{24,0},{1,9},{9,17},{17,25},{25,1},{2,10},{10... | collective-permute-start | bytes 1474568 | tf_op jit(solution)/shard_map/ppermute | solution.py:22
  782.7 18.7 %collective-permute-start.18 = (bf16[128,1920]{1,0:T(8,128)(2,1)}, bf16[128,1920]{1,0:T(8,128)(2,1)}, u32[]{:S(2)}, u32[]{:S(2)}) collective-permute-start(bf16[128,1920]{1,0:T(8,128)(2,1)} %slice.395), channel_id=1, source_target_pairs={{0,24},{8,0},{16,8},{24,16},{1,25},{9,1},{17,9},{25,17},{2,26},{10... | collective-permute-start | bytes 1474568 | tf_op jit(solution)/shard_map/ppermute | solution.py:26
  811.5 16.8 %collective-permute-start.35 = (bf16[4,4,64,375]{3,2,1,0:T(8,128)(2,1)}, bf16[4,4,64,375]{3,2,1,0:T(8,128)(2,1)}, u32[]{:S(2)}, u32[]{:S(2)}) collective-permute-start(bf16[4,4,64,375]{3,2,1,0:T(8,128)(2,1)} %fusion.32), channel_id=1, source_target_pairs={{0,1},{1,0},{2,3},{3,2},{4,5},{5,4},{6,7},{7,6},{8,9},{9,8},{10,11... | collective-permute-start | bytes 2304008 | tf_op jit(solution)/shard_map/ppermute | solution.py:192
  (39 other events, 100.8 us)
Sparse Core Ops, SparseCore 0:
  73.1 280.9 all-reduce.3
where the time goes:
time: 845 us; the launch traced here: 839 us
  blocking collectives  291 us (34%)
  waiting for transfers between devices  249 us (29%)
  matrix products  107 us (13%)
  local copies, waits for them, and re-layouts  85.2 us (10%)
  starting transfers between devices  57.4 us (7%)
  between operations  28.5 us (3%)
  other arithmetic  21.1 us (2%)
    unnamed x2, waiting for transfers between devices  221 us
    unnamed x1, blocking collectives  155 us
    dot_general x60, matrix products, dot(): return lax.dot_general(a, b, (dims, ((), ())), preferred_element_type=F32)  105 us
    psum x1, blocking collectives, local(): z_sum = lax.psum(z_part, ('x', 'z'))  70.3 us
    psum x1, blocking collectives, local(): density = lax.psum(jnp.stack(entries), OCC_AUX)  65.9 us
    ppermute x16, starting transfers between devices, down(): return lax.ppermute(v, axis, ring(4, -1))  45.5 us
    unnamed x108, local copies, waits for them, and re-layouts  43.4 us
    ppermute x16, waiting for transfers between devices, up(): return lax.ppermute(v, axis, ring(4, 1))  18.4 us
  transfers between devices with their start and end apart: 39, of which 10 were waited for; matrix products, arithmetic and copies ran while one was open for 22% of the time, Pallas kernels for 0%

commit v1 on v0

--- a/solution.py
+++ b/solution.py
@@ -132,7 +132,7 @@
             for k in range(KH)
         ]
     )
-    z_sum = lax.psum(z_part, ("x", "z"))
+    z_sum = lax.psum(lax.psum(z_part, "z"), "x")
 
     def by_block(left, swapped):
         blocks = left.reshape(4, 4, NI * PAD, nq)

time: 845 us -> 811 us (0.960)
  blocking collectives: 291 us -> 256 us
    psum x1 -> x2, blocking collectives: 70.3 us -> 36 us  [local(): z_sum = lax.psum(lax.psum(z_part, 'z'), 'x')]
  transfers between devices with their start and end apart: 39 -> 39, of which waited for: 10 -> 10; matrix products, arithmetic and copies ran while one was open for 22% -> 23% of each run, Pallas kernels for 0% -> 0%
where the time goes in v1:
time: 811 us; the launch traced here: 805 us
  blocking collectives  256 us (32%)
  waiting for transfers between devices  249 us (31%)
  matrix products  107 us (13%)
  local copies, waits for them, and re-layouts  84.8 us (10%)
  starting transfers between devices  58.1 us (7%)
  between operations  29 us (4%)
  other arithmetic  21.3 us (3%)
    unnamed x2, waiting for transfers between devices  221 us
    unnamed x1, blocking collectives  155 us
    dot_general x60, matrix products, dot(): return lax.dot_general(a, b, (dims, ((), ())), preferred_element_type=F32)  105 us
    psum x1, blocking collectives, local(): density = lax.psum(jnp.stack(entries), OCC_AUX)  65.8 us
    ppermute x16, starting transfers between devices, down(): return lax.ppermute(v, axis, ring(4, -1))  44.9 us
    unnamed x108, local copies, waits for them, and re-layouts  42.9 us
    psum x2, blocking collectives, local(): z_sum = lax.psum(lax.psum(z_part, 'z'), 'x')  36 us
    ppermute x16, waiting for transfers between devices, up(): return lax.ppermute(v, axis, ring(4, 1))  18.6 us
  transfers between devices with their start and end apart: 39, of which 10 were waited for; matrix products, arithmetic and copies ran while one was open for 23% of the time, Pallas kernels for 0%

profile of v1, /device:TPU:0, one launch (start us, length us, event | category | flops | bytes accessed | tf_op | source)
XLA Modules:
  0.0 805.0 jit_solution(3090655464387811991)
XLA Ops:
  10.6 2.6 dynamic-slice_bitcast_fusion
  18.7 2.5 fusion.101
  28.6 13.4 %fusion.165 = (bf16[1,375,4000]{2,0,1:T(2,128)(2,1)}, bf16[1,375,4000]{2,0,1:T(2,128)(2,1)}) fusion(bf16[2,375,4000]{2,0,1:T(2,128)(2,1)} %param.14), kind=kLoop, calls=%fused_computation.334 | loop fusion | bytes 12000000 | tf_op jit(solution)/shard_map/slice | solution.py:109
  42.0 13.8 %copy.135 = bf16[1,375,4000]{1,2,0:T(8,128)(2,1)S(1)} copy(bf16[1,375,4000]{2,0,1:T(2,128)(2,1)} %get-tuple-element.35) | data formatting | bytes 6000000
  56.8 13.9 %copy.134 = bf16[1,375,4000]{1,2,0:T(8,128)(2,1)S(1)} copy(bf16[1,375,4000]{2,0,1:T(2,128)(2,1)} %get-tuple-element.34) | data formatting | bytes 6000000
  77.3 2.5 fusion.98
  81.2 2.8 fusion.79
  84.0 2.7 fusion.81
  86.7 2.7 fusion.77
  89.5 2.7 fusion.71
  92.2 2.7 fusion.73
  94.9 2.7 fusion.75
  97.7 2.7 fusion.83
  100.4 2.7 fusion.85
  105.2 2.8 fusion.53
  107.9 2.8 fusion.55
  112.4 2.8 fusion.51
  115.2 2.8 fusion.45
  118.0 2.7 fusion.47
  120.7 2.8 fusion.49
  123.5 2.8 fusion.59
  129.1 2.7 fusion.57
  134.0 220.5 %all-reduce.4.cloned.1.call-done = f32[32,6,125]{2,1,0:T(8,128)} async-done(((f32[32,6,125]{2,1,0:T(8,128)}), f32[32,6,125]{2,1,0:T(8,128)}) %all-reduce.4.cloned.1.call-update) | async-done | bytes 96016
  356.5 154.6 %all-reduce.1 = f32[32,6,15]{2,1,0:T(8,128)S(1)} all-reduce(f32[32,6,15]{2,1,0:T(8,128)S(1)} %copy.133), channel_id=3, replica_groups=mesh['yh'=2,'core'=2,'x'=4,'z'=4,'yl'=2] {'x','z','yl'}, use_global_device_ids=true, to_apply=%region_11.12.clone | all-reduce | flops 2880 | bytes 23040
  520.4 3.2 collective-permute-start.5
  531.4 3.2 collective-permute-start.21
  537.9 21.0 %psum.21 = f32[2,4,1920]{2,1,0:T(4,128)S(1)} all-reduce(f32[2,4,1920]{2,1,0:T(4,128)S(1)} %pad_maximum_fusion.14), channel_id=1, replica_groups=mesh['yh'=2,'core'=2,'x'=4,'z'=4,'yl'=2] {'z'}, use_global_device_ids=true, to_apply=%region_0.1 | all-reduce | flops 15360 | bytes 122880 | tf_op jit(solution)/shard_map/psum | solution.py:135
  558.9 15.0 %psum.22 = f32[2,4,1920]{2,1,0:T(4,128)S(1)} all-reduce(f32[2,4,1920]{2,1,0:T(4,128)S(1)} %psum.21), channel_id=1, replica_groups=mesh['yh'=2,'core'=2,'x'=4,'z'=4,'yl'=2] {'x'}, use_global_device_ids=true, to_apply=%region_1.2 | all-reduce | flops 15360 | bytes 122880 | tf_op jit(solution)/shard_map/psum | solution.py:135
  587.0 2.7 collective-permute-start.22
  589.7 3.2 collective-permute-done.4
  595.0 3.2 collective-permute-start.9
  601.8 3.2 collective-permute-start.25
  605.8 3.3 collective-permute-start.10
  609.2 3.3 collective-permute-start.26
  613.1 3.5 collective-permute-done.24
  620.6 3.3 collective-permute-start.27
  624.6 2.6 collective-permute-start.11
  634.3 65.8 %psum.23 = f32[3]{0:T(128)S(1)} all-reduce(f32[3]{0:T(128)S(1)} %pad_maximum_fusion.17), channel_id=1, replica_groups=mesh['yh'=2,'core'=2,'x'=4,'z'=4,'yl'=2] {'yh','core','x','z','yl'}, use_global_device_ids=true, to_apply=%region_18.19 | all-reduce | flops 3 | bytes 24 | tf_op jit(solution)/shard_map/psum | solution.py:168
  718.2 2.6 collective-permute-start.31
  724.6 2.6 collective-permute-start.15
  727.2 3.1 fusion.43
  730.3 2.9 fusion.69
  734.4 7.1 collective-permute-done.32
  741.7 3.3 collective-permute-start.34
  749.0 3.2 collective-permute-start.18
  772.2 3.0 copy.121
  775.2 2.6 fusion.32
  787.6 6.9 collective-permute-done.35
  (299 shorter events, 134.3 us)
Async XLA Ops:
  7.2 7.7 copy-start.42
  7.2 347.3 %all-reduce.4.cloned.1.call-start = ((), (), s32[]{:S(2)}) async-start(), calls=%async_computation | async-start | bytes 262144
  13.2 113.1 %collective-permute-start.1 = (bf16[375,1920]{1,0:T(8,128)(2,1)}, bf16[375,1920]{1,0:T(8,128)(2,1)}, u32[]{:S(2)}, u32[]{:S(2)}) collective-permute-start(bf16[375,1920]{1,0:T(8,128)(2,1)} %dynamic-slice_bitcast_fusion), channel_id=1, source_target_pairs={{0,1},{1,0},{32,97},{33,96},{64,65},{65,64},{96,33},{97,32},{2,3},... | collective-permute-start | bytes 4320008 | tf_op jit(solution)/shard_map/ppermute | solution.py:82
  26.3 485.4 %collective-permute-start = (bf16[1024,375]{0,1:T(8,128)(2,1)}, bf16[1024,375]{0,1:T(8,128)(2,1)}, u32[]{:S(2)}, u32[]{:S(2)}) collective-permute-start(bf16[1024,375]{0,1:T(8,128)(2,1)} %copy.104), channel_id=1, source_target_pairs={{0,1},{1,0},{32,97},{33,96},{64,65},{65,64},{96,33},{97,32},{2,3},... | collective-permute-start | bytes 2304008 | tf_op jit(solution)/shard_map/ppermute | solution.py:82
  26.7 510.6 %collective-permute-start.36 = (bf16[4,375]{1,0:T(4,128)(2,1)S(1)}, bf16[4,375]{1,0:T(4,128)(2,1)S(1)}, u32[]{:S(2)}, u32[]{:S(2)}) collective-permute-start(bf16[4,375]{1,0:T(4,128)(2,1)S(1)} %reshape.436), channel_id=1, source_target_pairs={{0,1},{1,0},{2,3},{3,2},{4,5},{5,4},{6,7},{7,6},{8,9},{9,8},{10,11... | collective-permute-start | bytes 9008 | tf_op jit(solution)/shard_map/ppermute | solution.py:127
  126.3 387.9 %collective-permute-start.2 = (bf16[375,1920]{1,0:T(8,128)(2,1)}, bf16[375,1920]{1,0:T(8,128)(2,1)}, u32[]{:S(2)}, u32[]{:S(2)}) collective-permute-start(bf16[375,1920]{1,0:T(8,128)(2,1)} %collective-permute-done.1), channel_id=1, source_target_pairs={{0,32},{32,0},{1,33},{33,1},{2,34},{34,2},{3,35},{35,3},{4,36},{36... | collective-permute-start | bytes 4320008 | tf_op jit(solution)/shard_map/ppermute | solution.py:85
  514.1 21.9 %copy-start.25 = (bf16[4,4,64,375]{3,2,1,0:T(8,128)(2,1)}, bf16[4,4,64,375]{3,2,1,0:T(8,128)(2,1)S(1)}, u32[]{:S(2)}) copy-start(bf16[4,4,64,375]{3,2,1,0:T(8,128)(2,1)S(1)} %copy.118) | copy-start | bytes 2304004
  518.0 57.9 %collective-permute-start.3 = (bf16[128,1920]{1,0:T(8,128)(2,1)}, bf16[128,1920]{1,0:T(8,128)(2,1)}, u32[]{:S(2)}, u32[]{:S(2)}) collective-permute-start(bf16[128,1920]{1,0:T(8,128)(2,1)} %fusion.13), channel_id=1, source_target_pairs={{0,8},{8,16},{16,24},{24,0},{1,9},{9,17},{17,25},{25,1},{2,10},{10... | collective-permute-start | bytes 1474568 | tf_op jit(solution)/shard_map/ppermute | solution.py:22
  520.4 57.9 %collective-permute-start.5 = (bf16[128,1920]{1,0:T(8,128)(2,1)}, bf16[128,1920]{1,0:T(8,128)(2,1)}, u32[]{:S(2)}, u32[]{:S(2)}) collective-permute-start(bf16[128,1920]{1,0:T(8,128)(2,1)} %fusion.17), channel_id=1, source_target_pairs={{0,24},{8,0},{16,8},{24,16},{1,25},{9,1},{17,9},{25,17},{2,26},{10... | collective-permute-start | bytes 1474568 | tf_op jit(solution)/shard_map/ppermute | solution.py:26
  528.9 53.7 %collective-permute-start.19 = (bf16[128,1920]{1,0:T(8,128)(2,1)}, bf16[128,1920]{1,0:T(8,128)(2,1)}, u32[]{:S(2)}, u32[]{:S(2)}) collective-permute-start(bf16[128,1920]{1,0:T(8,128)(2,1)} %fusion.19), channel_id=1, source_target_pairs={{0,2},{2,4},{4,6},{6,0},{1,3},{3,5},{5,7},{7,1},{8,10},{10,12},{12... | collective-permute-start | bytes 1474568 | tf_op jit(solution)/shard_map/ppermute | solution.py:22
  531.4 53.4 %collective-permute-start.21 = (bf16[128,1920]{1,0:T(8,128)(2,1)}, bf16[128,1920]{1,0:T(8,128)(2,1)}, u32[]{:S(2)}, u32[]{:S(2)}) collective-permute-start(bf16[128,1920]{1,0:T(8,128)(2,1)} %fusion.23), channel_id=1, source_target_pairs={{0,6},{2,0},{4,2},{6,4},{1,7},{3,1},{5,3},{7,5},{8,14},{10,8},{12,... | collective-permute-start | bytes 1474568 | tf_op jit(solution)/shard_map/ppermute | solution.py:26
  577.6 15.4 %collective-permute-start.4 = (bf16[256,1920]{1,0:T(8,128)(2,1)S(1)}, bf16[256,1920]{1,0:T(8,128)(2,1)S(1)}, u32[]{:S(2)}, u32[]{:S(2)}) collective-permute-start(bf16[256,1920]{1,0:T(8,128)(2,1)S(1)} %pad_maximum_fusion.4), channel_id=1, source_target_pairs={{0,8},{8,16},{16,24},{24,0},{1,9},{9,17},{17,25},{25,1},{2,10},{10... | collective-permute-start | bytes 2949128 | tf_op jit(solution)/shard_map/ppermute | solution.py:22
  580.3 14.2 %collective-permute-start.6 = (bf16[256,1920]{1,0:T(8,128)(2,1)S(1)}, bf16[256,1920]{1,0:T(8,128)(2,1)S(1)}, u32[]{:S(2)}, u32[]{:S(2)}) collective-permute-start(bf16[256,1920]{1,0:T(8,128)(2,1)S(1)} %pad_maximum_fusion.5), channel_id=1, source_target_pairs={{0,24},{8,0},{16,8},{24,16},{1,25},{9,1},{17,9},{25,17},{2,26},{10... | collective-permute-start | bytes 2949128 | tf_op jit(solution)/shard_map/ppermute | solution.py:26
  584.3 15.8 %collective-permute-start.20 = (bf16[256,1920]{1,0:T(8,128)(2,1)S(1)}, bf16[256,1920]{1,0:T(8,128)(2,1)S(1)}, u32[]{:S(2)}, u32[]{:S(2)}) collective-permute-start(bf16[256,1920]{1,0:T(8,128)(2,1)S(1)} %pad_maximum_fusion.6), channel_id=1, source_target_pairs={{0,2},{2,4},{4,6},{6,0},{1,3},{3,5},{5,7},{7,1},{8,10},{10,12},{12... | collective-permute-start | bytes 2949128 | tf_op jit(solution)/shard_map/ppermute | solution.py:22
  586.9 7.6 copy-start.23
  586.9 7.5 copy-start.24
  587.0 14.3 %collective-permute-start.22 = (bf16[256,1920]{1,0:T(8,128)(2,1)S(1)}, bf16[256,1920]{1,0:T(8,128)(2,1)S(1)}, u32[]{:S(2)}, u32[]{:S(2)}) collective-permute-start(bf16[256,1920]{1,0:T(8,128)(2,1)S(1)} %pad_maximum_fusion.7), channel_id=1, source_target_pairs={{0,6},{2,0},{4,2},{6,4},{1,7},{3,1},{5,3},{7,5},{8,14},{10,8},{12,... | collective-permute-start | bytes 2949128 | tf_op jit(solution)/shard_map/ppermute | solution.py:26
  594.9 6.5 copy-start.19
  594.9 10.1 %collective-permute-start.7 = (bf16[32,1920]{1,0:T(8,128)(2,1)S(1)}, bf16[32,1920]{1,0:T(8,128)(2,1)S(1)}, u32[]{:S(2)}, u32[]{:S(2)}) collective-permute-start(bf16[32,1920]{1,0:T(8,128)(2,1)S(1)} %get-tuple-element.50), channel_id=1, source_target_pairs={{0,2},{2,4},{4,6},{6,0},{1,3},{3,5},{5,7},{7,1},{8,10},{10,12},{12... | collective-permute-start | bytes 368648 | tf_op jit(solution)/shard_map/ppermute | solution.py:22
  595.0 10.1 %collective-permute-start.9 = (bf16[32,1920]{1,0:T(8,128)(2,1)S(1)}, bf16[32,1920]{1,0:T(8,128)(2,1)S(1)}, u32[]{:S(2)}, u32[]{:S(2)}) collective-permute-start(bf16[32,1920]{1,0:T(8,128)(2,1)S(1)} %get-tuple-element.51), channel_id=1, source_target_pairs={{0,6},{2,0},{4,2},{6,4},{1,7},{3,1},{5,3},{7,5},{8,14},{10,8},{12,... | collective-permute-start | bytes 368648 | tf_op jit(solution)/shard_map/ppermute | solution.py:26
  601.8 7.3 collective-permute-start.23
  601.8 7.2 collective-permute-start.25
  605.2 7.9 collective-permute-start.8
  605.8 7.3 collective-permute-start.10
  609.1 7.5 collective-permute-start.24
  609.2 7.4 collective-permute-start.26
  620.6 83.2 %collective-permute-start.27 = (bf16[64,1920]{1,0:T(8,128)(2,1)}, bf16[64,1920]{1,0:T(8,128)(2,1)}, u32[]{:S(2)}, u32[]{:S(2)}) collective-permute-start(bf16[64,1920]{1,0:T(8,128)(2,1)} %get-tuple-element.30), channel_id=1, source_target_pairs={{0,24},{8,0},{16,8},{24,16},{1,25},{9,1},{17,9},{25,17},{2,26},{10... | collective-permute-start | bytes 737288 | tf_op jit(solution)/shard_map/ppermute | solution.py:26
  623.9 77.0 %collective-permute-start.28 = (bf16[64,1920]{1,0:T(8,128)(2,1)}, bf16[64,1920]{1,0:T(8,128)(2,1)}, u32[]{:S(2)}, u32[]{:S(2)}) collective-permute-start(bf16[64,1920]{1,0:T(8,128)(2,1)} %get-tuple-element.30), channel_id=1, source_target_pairs={{0,8},{8,16},{16,24},{24,0},{1,9},{9,17},{17,25},{25,1},{2,10},{10... | collective-permute-start | bytes 737288 | tf_op jit(solution)/shard_map/ppermute | solution.py:22
  624.6 84.3 %collective-permute-start.11 = (bf16[64,1920]{1,0:T(8,128)(2,1)S(1)}, bf16[64,1920]{1,0:T(8,128)(2,1)}, u32[]{:S(2)}, u32[]{:S(2)}) collective-permute-start(bf16[64,1920]{1,0:T(8,128)(2,1)S(1)} %get-tuple-element.58), channel_id=1, source_target_pairs={{0,6},{2,0},{4,2},{6,4},{1,7},{3,1},{5,3},{7,5},{8,14},{10,8},{12,... | collective-permute-start | bytes 737288 | tf_op jit(solution)/shard_map/ppermute | solution.py:26
  627.2 78.9 %collective-permute-start.12 = (bf16[64,1920]{1,0:T(8,128)(2,1)S(1)}, bf16[64,1920]{1,0:T(8,128)(2,1)}, u32[]{:S(2)}, u32[]{:S(2)}) collective-permute-start(bf16[64,1920]{1,0:T(8,128)(2,1)S(1)} %get-tuple-element.58), channel_id=1, source_target_pairs={{0,2},{2,4},{4,6},{6,0},{1,3},{3,5},{5,7},{7,1},{8,10},{10,12},{12... | collective-permute-start | bytes 737288 | tf_op jit(solution)/shard_map/ppermute | solution.py:22
  634.3 66.0 %collective-permute-start.37 = (f32[2,15]{1,0:T(2,128)S(1)}, f32[2,15]{1,0:T(2,128)S(1)}, u32[]{:S(2)}, u32[]{:S(2)}) collective-permute-start(f32[2,15]{1,0:T(2,128)S(1)} %constant_dynamic-slice_fusion), channel_id=1, source_target_pairs={{0,1},{1,0},{2,3},{3,2},{4,5},{5,4},{6,7},{7,6},{8,9},{9,8},{10,11... | collective-permute-start | bytes 368 | tf_op jit(solution)/shard_map/ppermute | solution.py:179
  701.8 12.8 %collective-permute-start.29 = (bf16[32,1920]{1,0:T(8,128)(2,1)S(1)}, bf16[32,1920]{1,0:T(8,128)(2,1)S(1)}, u32[]{:S(2)}, u32[]{:S(2)}) collective-permute-start(bf16[32,1920]{1,0:T(8,128)(2,1)S(1)} %slice.420), channel_id=1, source_target_pairs={{0,8},{8,16},{16,24},{24,0},{1,9},{9,17},{17,25},{25,1},{2,10},{10... | collective-permute-start | bytes 368648 | tf_op jit(solution)/shard_map/ppermute | solution.py:22
  704.6 10.6 %collective-permute-start.30 = (bf16[32,1920]{1,0:T(8,128)(2,1)S(1)}, bf16[32,1920]{1,0:T(8,128)(2,1)S(1)}, u32[]{:S(2)}, u32[]{:S(2)}) collective-permute-start(bf16[32,1920]{1,0:T(8,128)(2,1)S(1)} %slice.421), channel_id=1, source_target_pairs={{0,24},{8,0},{16,8},{24,16},{1,25},{9,1},{17,9},{25,17},{2,26},{10... | collective-permute-start | bytes 368648 | tf_op jit(solution)/shard_map/ppermute | solution.py:26
  707.0 13.8 %collective-permute-start.13 = (bf16[32,1920]{1,0:T(8,128)(2,1)S(1)}, bf16[32,1920]{1,0:T(8,128)(2,1)S(1)}, u32[]{:S(2)}, u32[]{:S(2)}) collective-permute-start(bf16[32,1920]{1,0:T(8,128)(2,1)S(1)} %slice.392), channel_id=1, source_target_pairs={{0,2},{2,4},{4,6},{6,0},{1,3},{3,5},{5,7},{7,1},{8,10},{10,12},{12... | collective-permute-start | bytes 368648 | tf_op jit(solution)/shard_map/ppermute | solution.py:22
  709.8 11.7 %collective-permute-start.14 = (bf16[32,1920]{1,0:T(8,128)(2,1)S(1)}, bf16[32,1920]{1,0:T(8,128)(2,1)S(1)}, u32[]{:S(2)}, u32[]{:S(2)}) collective-permute-start(bf16[32,1920]{1,0:T(8,128)(2,1)S(1)} %slice.393), channel_id=1, source_target_pairs={{0,6},{2,0},{4,2},{6,4},{1,7},{3,1},{5,3},{7,5},{8,14},{10,8},{12,... | collective-permute-start | bytes 368648 | tf_op jit(solution)/shard_map/ppermute | solution.py:26
  717.6 23.9 %collective-permute-start.32 = (bf16[256,1920]{1,0:T(8,128)(2,1)}, bf16[256,1920]{1,0:T(8,128)(2,1)S(1)}, u32[]{:S(2)}, u32[]{:S(2)}) collective-permute-start(bf16[256,1920]{1,0:T(8,128)(2,1)} %constant_dynamic-update-slice_fusion.7), channel_id=1, source_target_pairs={{0,2},{2,4},{4,6},{6,0},{1,3},{3,5},{5,7},{7,1},{8,10},{10,12},{12... | collective-permute-start | bytes 2949128 | tf_op jit(solution)/shard_map/ppermute | solution.py:22
  718.2 23.4 %collective-permute-start.31 = (bf16[256,1920]{1,0:T(8,128)(2,1)}, bf16[256,1920]{1,0:T(8,128)(2,1)S(1)}, u32[]{:S(2)}, u32[]{:S(2)}) collective-permute-start(bf16[256,1920]{1,0:T(8,128)(2,1)} %constant_dynamic-update-slice_fusion.7), channel_id=1, source_target_pairs={{0,6},{2,0},{4,2},{6,4},{1,7},{3,1},{5,3},{7,5},{8,14},{10,8},{12,... | collective-permute-start | bytes 2949128 | tf_op jit(solution)/shard_map/ppermute | solution.py:26
  723.8 6.5 copy-start.6
  723.8 23.5 %collective-permute-start.16 = (bf16[256,1920]{1,0:T(8,128)(2,1)}, bf16[256,1920]{1,0:T(8,128)(2,1)S(1)}, u32[]{:S(2)}, u32[]{:S(2)}) collective-permute-start(bf16[256,1920]{1,0:T(8,128)(2,1)} %constant_dynamic-update-slice_fusion), channel_id=1, source_target_pairs={{0,8},{8,16},{16,24},{24,0},{1,9},{9,17},{17,25},{25,1},{2,10},{10... | collective-permute-start | bytes 2949128 | tf_op jit(solution)/shard_map/ppermute | solution.py:22
  724.6 23.5 %collective-permute-start.15 = (bf16[256,1920]{1,0:T(8,128)(2,1)}, bf16[256,1920]{1,0:T(8,128)(2,1)S(1)}, u32[]{:S(2)}, u32[]{:S(2)}) collective-permute-start(bf16[256,1920]{1,0:T(8,128)(2,1)} %constant_dynamic-update-slice_fusion), channel_id=1, source_target_pairs={{0,24},{8,0},{16,8},{24,16},{1,25},{9,1},{17,9},{25,17},{2,26},{10... | collective-permute-start | bytes 2949128 | tf_op jit(solution)/shard_map/ppermute | solution.py:26
  727.2 6.0 copy-start.5
  730.3 25.9 %slice-start = ((s8[8663040]{0:T(1024)(128)(4,1)}), s8[4194304]{0:T(1024)(128)(4,1)S(1)}, s32[]{:S(2)}) async-start(s8[8663040]{0:T(1024)(128)(4,1)} %bitcast.415), calls=%async_computation.1 | async-start | bytes 8388608
  733.8 22.4 %slice-start.1 = ((s8[8663040]{0:T(1024)(128)(4,1)}), s8[4194304]{0:T(1024)(128)(4,1)S(1)}, s32[]{:S(2)}) async-start(s8[8663040]{0:T(1024)(128)(4,1)} %bitcast.415), calls=%async_computation.2 | async-start | bytes 8388608
  741.6 20.1 %collective-permute-start.33 = (bf16[128,1920]{1,0:T(8,128)(2,1)S(1)}, bf16[128,1920]{1,0:T(8,128)(2,1)S(1)}, u32[]{:S(2)}, u32[]{:S(2)}) collective-permute-start(bf16[128,1920]{1,0:T(8,128)(2,1)S(1)} %slice.422), channel_id=1, source_target_pairs={{0,2},{2,4},{4,6},{6,0},{1,3},{3,5},{5,7},{7,1},{8,10},{10,12},{12... | collective-permute-start | bytes 1474568 | tf_op jit(solution)/shard_map/ppermute | solution.py:22
  741.7 20.0 %collective-permute-start.34 = (bf16[128,1920]{1,0:T(8,128)(2,1)S(1)}, bf16[128,1920]{1,0:T(8,128)(2,1)S(1)}, u32[]{:S(2)}, u32[]{:S(2)}) collective-permute-start(bf16[128,1920]{1,0:T(8,128)(2,1)S(1)} %slice.423), channel_id=1, source_target_pairs={{0,6},{2,0},{4,2},{6,4},{1,7},{3,1},{5,3},{7,5},{8,14},{10,8},{12,... | collective-permute-start | bytes 1474568 | tf_op jit(solution)/shard_map/ppermute | solution.py:26
  748.2 18.4 %collective-permute-start.17 = (bf16[128,1920]{1,0:T(8,128)(2,1)}, bf16[128,1920]{1,0:T(8,128)(2,1)}, u32[]{:S(2)}, u32[]{:S(2)}) collective-permute-start(bf16[128,1920]{1,0:T(8,128)(2,1)} %slice.394), channel_id=1, source_target_pairs={{0,8},{8,16},{16,24},{24,0},{1,9},{9,17},{17,25},{25,1},{2,10},{10... | collective-permute-start | bytes 1474568 | tf_op jit(solution)/shard_map/ppermute | solution.py:22
  749.0 18.7 %collective-permute-start.18 = (bf16[128,1920]{1,0:T(8,128)(2,1)}, bf16[128,1920]{1,0:T(8,128)(2,1)}, u32[]{:S(2)}, u32[]{:S(2)}) collective-permute-start(bf16[128,1920]{1,0:T(8,128)(2,1)} %slice.395), channel_id=1, source_target_pairs={{0,24},{8,0},{16,8},{24,16},{1,25},{9,1},{17,9},{25,17},{2,26},{10... | collective-permute-start | bytes 1474568 | tf_op jit(solution)/shard_map/ppermute | solution.py:26
  777.8 16.8 %collective-permute-start.35 = (bf16[4,4,64,375]{3,2,1,0:T(8,128)(2,1)}, bf16[4,4,64,375]{3,2,1,0:T(8,128)(2,1)}, u32[]{:S(2)}, u32[]{:S(2)}) collective-permute-start(bf16[4,4,64,375]{3,2,1,0:T(8,128)(2,1)} %fusion.32), channel_id=1, source_target_pairs={{0,1},{1,0},{2,3},{3,2},{4,5},{5,4},{6,7},{7,6},{8,9},{9,8},{10,11... | collective-permute-start | bytes 2304008 | tf_op jit(solution)/shard_map/ppermute | solution.py:192
  (39 other events, 101.1 us)
Sparse Core Ops, SparseCore 0:
  73.5 280.9 all-reduce.3
